TPU v7x, 128 devices: a whole 4x4x4 slice. The times are simulated.
128 devices in a mesh: row: 8 (over y, core), col: 16 (over z, x).
Axes of the slice: x: 4, y: 4, z: 4, core: 2. Of those that a mesh axis runs over, the one named last changes fastest.
Arguments:
- amplitudes: float32 [16384, 4096], P('row', 'col'), may hold values from -6 to 6
- integrals: float32 [4096, 16384], P('row', 'col'), may hold values from -0.09375 to 0.09375
- amp_mask: int32 [256, 64], P('row', 'col'), may hold values 0 or 1
- int_mask: int32 [64, 256], P('row', 'col'), may hold values 0 or 1
- occ_shift: float32 [16384], P('row'), may hold values from 0.5 to 4
- virt_shift: float32 [16384], P('col'), may hold values from 0.5 to 4
Outputs:
- update: float32 [16384, 16384], P(None, ('col', 'row'))
All inputs are finite; a program needn't handle non-finite values. No bound on the sum of `amp_mask` or of `int_mask` on one device may be relied on, other than what follows from the above.
Results may differ from a plain program's by a relative error of at most 0.00007.
Values sent between devices are 32-bit elements; how exact they have to be, the bound alone decides.
A program may use at most 192 MiB of HBM per device.

v0:
```python
import jax
import jax.numpy as jnp
from jax import lax
from jax.sharding import PartitionSpec as P

TILE = 64


def apply_mask(block, mask):
    rows, cols = block.shape
    tiled = block.reshape(rows // TILE, TILE, cols // TILE, TILE)
    tiled = tiled * mask.astype(jnp.float32)[:, None, :, None]
    return tiled.reshape(rows, cols)


def shards(amplitudes, integrals, amp_mask, int_mask, occ_shift, virt_shift):
    masked_amps = apply_mask(amplitudes, amp_mask)
    masked_ints = apply_mask(integrals, int_mask)
    whole_ints = lax.all_gather(masked_ints, "row", axis=0, tiled=True)
    ladder = jnp.dot(
        lax.all_gather(masked_amps, "col", axis=1, tiled=True),
        whole_ints,
        precision=lax.Precision.HIGHEST,
        preferred_element_type=jnp.float32,
    )
    scaled = ladder / (occ_shift[:, None] + virt_shift[None, :])
    return lax.all_to_all(scaled, "row", split_axis=1, concat_axis=0, tiled=True)


def solution(mesh):
    placed = (
        P("row", "col"),
        P("row", "col"),
        P("row", "col"),
        P("row", "col"),
        P("row"),
        P("col"),
    )
    return jax.shard_map(
        shards, mesh=mesh, in_specs=placed, out_specs=P(None, ("col", "row")), check_vma=False
    )
```

profile of v0, /device:TPU:1, one launch (start us, length us, event | category | flops | bytes accessed | tf_op | source)
XLA Modules:
  0.0 545.7 jit_solution(8266703104543538418)
XLA Ops:
  6.5 0.0 all-gather.5.cloned.1.call-start
  6.5 0.7 convert_element_type.7
  7.2 2.4 mul.25
  9.6 0.0 copy-start
  9.6 3.5 mul.26
  13.1 3.3 mul.27
  16.4 0.0 all-gather.5.cloned.1.call-update
  16.5 0.0 all-gather.3.cloned.1.call-start
  16.5 0.0 copy-done
  16.5 0.1 copy.7
  16.6 2.6 mul.22
  19.2 0.0 copy-start.1
  19.2 0.0 copy-start.2
  19.2 4.2 mul.23
  23.4 3.2 mul.24
  26.6 0.0 all-gather.3.cloned.1.call-update
  26.6 78.6 %all-gather.5.cloned.1.call-done = f32[4096,1024]{1,0:T(8,128)} async-done(((f32[512,1024]{1,0:T(8,128)}), f32[4096,1024]{1,0:T(8,128)}) %all-gather.5.cloned.1.call-update) | async-done | bytes 16777232 | tf_op jit(solution)/shard_map/all_gather | solution.py:19
  105.2 208.1 %all-gather.3.cloned.1.call-done = f32[2048,4096]{1,0:T(8,128)} async-done(((f32[2048,256]{1,0:T(8,128)}), f32[2048,4096]{1,0:T(8,128)}) %all-gather.3.cloned.1.call-update) | async-done | bytes 33554448 | tf_op jit(solution)/shard_map/all_gather | solution.py:21
  313.3 0.0 copy-done.1
  313.3 0.0 copy-done.2
  313.3 114.3 %add_divide_fusion = f32[2048,1024]{0,1:T(8,128)} fusion(f32[2048,4096]{1,0:T(8,128)} %all-gather.3.cloned.1.call-done, f32[4096,1024]{1,0:T(8,128)} %all-gather.5.cloned.1.call-done, f32[1024]{0:T(1024)S(1)} %copy-done.2, f32[2048]{0:T(1024)S(1)} %copy-done.1), kind=kOutput, calls=%fused_computation | convolution fusion | flops 103083409408 | bytes 58732544 | tf_op jit(solution)/shard_map/dot_general | solution.py:20
  427.6 102.1 %all_to_all.19 = f32[2048,8,128]{0,2,1:T(8,128)} all-to-all(f32[2048,8,128]{0,2,1:T(8,128)} %bitcast.8), channel_id=1, replica_groups=mesh['row'=8,'col'=16] {'row'}, dimensions={1} | all-to-all | bytes 16777216 | tf_op jit(solution)/shard_map/all_to_all | solution.py:27
  529.7 9.1 %copy.8 = f32[8,2048,128]{2,1,0:T(8,128)} copy(f32[8,2048,128]{1,2,0:T(8,128)} %bitcast.7) | data formatting | bytes 16777216 | tf_op jit(solution)/shard_map/all_to_all | solution.py:27
  (1 shorter events, 0.0 us)
Async XLA Ops:
  6.5 98.7 %all-gather.5.cloned.1.call-start = ((), (), s32[]{:S(2)}) async-start(), calls=%async_computation.2 | async-start | bytes 18874368 | tf_op jit(solution)/shard_map/all_gather | solution.py:19
  9.6 6.9 %copy-start = (s32[32,4]{0,1:T(4,128)S(1)}, s32[32,4]{0,1:T(4,128)}, u32[]{:S(2)}) copy-start(s32[32,4]{0,1:T(4,128)} %param.8) | copy-start | bytes 1540
  16.5 296.8 %all-gather.3.cloned.1.call-start = ((), (), s32[]{:S(2)}) async-start(), calls=%async_computation.1 | async-start | bytes 35651584 | tf_op jit(solution)/shard_map/all_gather | solution.py:21
  19.2 294.1 %copy-start.1 = (f32[2048]{0:T(1024)S(1)}, f32[2048]{0:T(1024)}, u32[]{:S(2)}) copy-start(f32[2048]{0:T(1024)} %param.10) | copy-start | bytes 24580
  19.2 294.1 %copy-start.2 = (f32[1024]{0:T(1024)S(1)}, f32[1024]{0:T(1024)}, u32[]{:S(2)}) copy-start(f32[1024]{0:T(1024)} %param.11) | copy-start | bytes 12292
Sparse Core Ops, SparseCore 0:
  16.6 88.5 all-gather.4
  107.3 205.9 all-gather.2
where the time goes:
time: 546 us
  waiting for transfers between devices  287 us (53%)
  matrix products  114 us (21%)
  blocking collectives  102 us (19%)
  local copies, waits for them, and re-layouts  21.9 us (4%)
  between operations  13.4 us (2%)
  other arithmetic  7.21 us (1%)
    all_gather x1, waiting for transfers between devices, shards(): lax.all_gather(masked_amps, 'col', axis=1, tiled=True)  208 us
    dot_general x1, matrix products, shards(): jnp.dot(lax.all_gather(masked_amps, 'col', axis=1, tiled=True), whole_int...  114 us
    all_to_all x1, blocking collectives, shards(): lax.all_to_all(scaled, 'row', split_axis=1, concat_axis=0, tiled=True)  102 us
    all_gather x1, waiting for transfers between devices, shards(): whole_ints = lax.all_gather(masked_ints, 'row', axis=0, tiled=True)  78.6 us
    mul x4, local copies, waits for them, and re-layouts, apply_mask(): tiled = tiled * mask.astype(jnp.float32)[:, None, :, None]  12.7 us
  transfers between devices with their start and end apart: 2, of which 2 were waited for; matrix products, arithmetic and copies ran while one was open for 2% of the time, Pallas kernels for 0%

commit v1 on v0

v1 whole, which is shorter than its diff:
```python
import functools

import jax
import jax.numpy as jnp
from jax import lax
from jax.experimental import pallas as pl
from jax.experimental.pallas import tpu as pltpu
from jax.sharding import PartitionSpec as P

MESH = pl.DeviceIdType.MESH
F32, BF16 = jnp.float32, jnp.bfloat16
TILE = 64
ROWS, DEPTH, COLS = 2048, 4096, 1024
CHUNK = 128
CHUNKS = ROWS // CHUNK
HALF = CHUNK // 2
PIECE = 64
PIECES = 512 // PIECE
AHEAD = 5
CATCH = 2 * AHEAD
WIDE = 512


def wait_bytes(ref, sem):
    pltpu.make_async_copy(ref, ref, sem).wait()


def kernel(
    amps, ints, amp_gain, int_gain, occ, virt,
    out, whole_amps,
    own, whole_ints, high, low, chunk_in, split, stage,
    amp_send, amp_recv, int_send, int_recv, sib_send, sib_recv, out_send, out_recv, local, load,
):
    row, col = lax.axis_index("row"), lax.axis_index("col")
    y, core = row // 2, row % 2
    z, x = col // 4, col % 4

    def at(dy=0, dz=0, dx=0, dcore=0):
        r = lax.rem(y + dy, 4) * 2 + lax.rem(core + dcore, 2)
        return r, lax.rem(z + dz, 4) * 4 + lax.rem(x + dx, 4)

    sibling = at(dcore=1)
    y_next, y_prev = at(dy=1), at(dy=3)
    x_near = (at(dx=1), at(dx=3))
    z_near = (at(dz=1), at(dz=3))
    first, second = (x_near, z_near), (z_near, x_near)
    partners = [*x_near, *z_near, sibling] + [at(dy=d, dcore=c) for d in (1, 2, 3) for c in (0, 1)]

    barrier = pltpu.get_barrier_semaphore()
    for partner in partners:
        pl.semaphore_signal(barrier, inc=1, device_id=partner, device_id_type=MESH)
    pl.semaphore_wait(barrier, len(partners))

    def remote(src, dst, send, recv, device):
        pltpu.make_async_remote_copy(
            src_ref=src, dst_ref=dst, send_sem=send, recv_sem=recv, device_id=device, device_id_type=MESH
        ).start()

    def rows_of(c, part=None):
        if part is None:
            return pl.ds(pl.multiple_of(c * CHUNK, CHUNK), CHUNK)
        return pl.ds(pl.multiple_of(c * CHUNK + part * HALF, HALF), HALF)

    def block(way, dz, dx, rows):
        return whole_amps.at[way, lax.rem(z + dz, 4), lax.rem(x + dx, 4), rows, :]

    def bundle(way, d, rows):
        if way == 0:
            return whole_amps.at[0, lax.rem(z + d, 4), :, rows, :]
        return whole_amps.at[1, :, lax.rem(x + d, 4), rows, :]

    def near(way, d, rows):
        return block(way, 0, d, rows) if way == 0 else block(way, d, 0, rows)

    def step1(c):
        rows = rows_of(c)
        for way in (0, 1):
            for e in (0, 1):
                remote(own.at[way, rows, :], block(way, 0, 0, rows), amp_send.at[way, 0, e], amp_recv.at[way, 0, e, c], first[way][e])

    def step2(c):
        for way in (0, 1):
            for e in (0, 1):
                d = 3 if e == 0 else 1
                wait_bytes(near(way, d, rows_of(c)), amp_recv.at[way, 0, e, c])
                part = near(way, d, rows_of(c, e))
                remote(part, part, amp_send.at[way, 1, e], amp_recv.at[way, 1, e, c], first[way][e])

    def step3(c):
        for way in (0, 1):
            for e in (0, 1):
                wait_bytes(near(way, 2, rows_of(c, e)), amp_recv.at[way, 1, e, c])
            line = bundle(way, 0, rows_of(c))
            for e in (0, 1):
                remote(line, line, amp_send.at[way, 2, e], amp_recv.at[way, 2, e, c], second[way][e])

    def step4(c):
        for way in (0, 1):
            for e in (0, 1):
                d = 3 if e == 0 else 1
                wait_bytes(bundle(way, d, rows_of(c)), amp_recv.at[way, 2, e, c])
                part = bundle(way, d, rows_of(c, e))
                remote(part, part, amp_send.at[way, 3, e], amp_recv.at[way, 3, e, c], second[way][e])

    def step5(c):
        for way in (0, 1):
            for e in (0, 1):
                wait_bytes(bundle(way, 2, rows_of(c, e)), amp_recv.at[way, 3, e, c])

    def tick(t):
        for lead, step in ((4, step1), (3, step2), (2, step3), (1, step4), (0, step5)):
            c = t + lead
            pl.when((c >= (4 if lead == 4 else 0)) & (c < CHUNKS))(functools.partial(step, c))

    def int_rows(p, part=None):
        if part is None:
            return pl.ds(pl.multiple_of(p * PIECE, PIECE), PIECE)
        return pl.ds(pl.multiple_of(p * PIECE + part * (PIECE // 2), PIECE // 2), PIECE // 2)

    def int_block(dy, dcore, rows):
        return whole_ints.at[lax.rem(y + dy, 4) * 2 + lax.rem(core + dcore, 2), rows, :]

    def halve(dy, dcore, rows_at, count):
        b = lax.rem(y + dy, 4) * 2 + lax.rem(core + dcore, 2)
        value = whole_ints[b, pl.ds(rows_at, count), :]
        top = value.astype(BF16)
        rows = pl.ds(pl.multiple_of(b * 512 + rows_at, count), count)
        high[rows, :] = top
        low[rows, :] = (value - top.astype(F32)).astype(BF16)

    def int_start(p):
        rows = int_rows(p)
        piece = int_block(0, 0, rows)
        remote(piece, piece, int_send.at[0], int_recv.at[0, p], y_next)
        remote(piece, piece, int_send.at[1], int_recv.at[1, p], y_prev)
        remote(piece, piece, sib_send, sib_recv.at[0, p], sibling)

    def int_pass(p):
        rows = int_rows(p)
        for e, d, device in ((0, 3, y_next), (1, 1, y_prev)):
            piece = int_block(d, 0, rows)
            wait_bytes(piece, int_recv.at[e, p])
            part = int_block(d, 0, int_rows(p, e))
            remote(part, part, int_send.at[2 + e], int_recv.at[2 + e, p], device)
            remote(piece, piece, sib_send, sib_recv.at[1 + e, p], sibling)

    def int_near(p):
        base = pl.multiple_of(p * PIECE, PIECE)
        halve(0, 0, base, PIECE)
        halve(3, 0, base, PIECE)
        halve(1, 0, base, PIECE)

    def int_sibling(p):
        rows, base = int_rows(p), pl.multiple_of(p * PIECE, PIECE)
        for k, d in ((0, 0), (1, 3), (2, 1)):
            wait_bytes(int_block(d, 1, rows), sib_recv.at[k, p])
            halve(d, 1, base, PIECE)

    def int_far(p):
        rows, base = int_rows(p), pl.multiple_of(p * PIECE, PIECE)
        for e in (0, 1):
            wait_bytes(int_block(2, 0, int_rows(p, e)), int_recv.at[2 + e, p])
        piece = int_block(2, 0, rows)
        remote(piece, piece, sib_send, sib_recv.at[3, p], sibling)
        halve(2, 0, base, PIECE)

    def int_far_sibling(p):
        wait_bytes(int_block(2, 1, int_rows(p)), sib_recv.at[3, p])
        halve(2, 1, pl.multiple_of(p * PIECE, PIECE), PIECE)

    def mask_chunk(c):
        for k in range(CHUNK // TILE):
            rows = pl.ds(pl.multiple_of(c * CHUNK + k * TILE, TILE), TILE)
            gain = amp_gain[pl.ds(c * (CHUNK // TILE) + k, 1), :]
            value = amps[rows, :] * gain
            own[0, rows, :] = value[:, :128]
            own[1, rows, :] = value[:, 128:]

    for c in range(4):
        mask_chunk(c)
        step1(c)

    @pl.loop(0, PIECES)
    def _(p):
        rows = int_rows(p)
        whole_ints[row, rows, :] = ints[rows, :] * int_gain[pl.ds(p, 1), :]
        int_start(p)

    @pl.loop(4, CHUNKS)
    def _(c):
        mask_chunk(c)

    for way in (0, 1):
        pltpu.make_async_copy(own.at[way], whole_amps.at[way, z, x], local.at[way]).start()
    for way in (0, 1):
        pltpu.make_async_copy(own.at[way], whole_amps.at[way, z, x], local.at[way]).wait()

    @pl.loop(0, 3)
    def _(t):
        tick(t - 3)

    @pl.loop(0, AHEAD - 1)
    def _(t):
        tick(t)
        for q in (0, 1):
            int_pass(2 * t + q)
        for q in (0, 1):
            int_near(2 * t + q)

        @pl.when(t > 0)
        def _():
            for q in (0, 1):
                int_sibling(2 * t - 2 + q)

    tick(AHEAD - 1)
    for q in (0, 1):
        int_sibling(2 * (AHEAD - 2) + q)

    @pl.loop(0, PIECES // 2)
    def _(p):
        int_far(p)

    tick(AHEAD)

    @pl.loop(PIECES // 2, PIECES)
    def _(p):
        int_far(p)
        int_far_sibling(p - PIECES // 2)

    @pl.loop(PIECES // 2, PIECES)
    def _(p):
        int_far_sibling(p)

    def fetch(c):
        slot = lax.rem(c, 2)
        return pltpu.make_async_copy(whole_amps.at[:, :, :, rows_of(c), :], chunk_in.at[slot], load.at[slot])

    @pl.loop(0, CHUNKS)
    def _(c):
        @pl.when((c > 0) & ((c >= CATCH) | (lax.rem(c, 2) == 0)))
        def _():
            tick(jnp.where(c < CATCH, AHEAD + c // 2, c))

        @pl.when((c == 0) | (c >= CATCH))
        def _():
            fetch(c).start()

        fetch(c).wait()

        @pl.when(c < CATCH - 1)
        def _():
            fetch(c + 1).start()

        slot = lax.rem(c, 2)

        @pl.loop(0, 16)
        def _(k):
            value = jnp.concatenate([chunk_in[slot, 0, k // 4, lax.rem(k, 4)], chunk_in[slot, 1, k // 4, lax.rem(k, 4)]], axis=1)
            top = value.astype(BF16)
            at_k = pl.ds(pl.multiple_of(k * 256, 256), 256)
            split[pl.ds(0, CHUNK), at_k] = top
            split[pl.ds(CHUNK, CHUNK), at_k] = (value - top.astype(F32)).astype(BF16)

        rows = rows_of(c)

        @pl.loop(0, COLS // WIDE)
        def _(n):
            wide = pl.ds(pl.multiple_of(n * WIDE, WIDE), WIDE)
            both = jnp.dot(split[...], high[:, wide], preferred_element_type=F32)
            rest = jnp.dot(split[pl.ds(0, CHUNK)], low[:, wide], preferred_element_type=F32)
            scaled = (both[:CHUNK] + (both[CHUNK:] + rest)) / (occ[rows, :] + virt[:, wide])
            for q in range(WIDE // 128):
                stage[n * (WIDE // 128) + q, rows, :] = scaled[:, q * 128:(q + 1) * 128]

        there = pl.ds(pl.multiple_of(row * ROWS + c * CHUNK, CHUNK), CHUNK)
        for d in (4, 5, 2, 3, 6, 7, 1):
            owner = lax.rem(row + d, 8)
            remote(stage.at[owner, rows, :], out.at[there, :], out_send, out_recv.at[row], (owner, col))
        pltpu.make_async_copy(stage.at[row, rows, :], out.at[there, :], out_recv.at[row]).start()

    for source in range(8):
        wait_bytes(out.at[pl.ds(source * ROWS, ROWS), :], out_recv.at[source])
    wait_bytes(stage.at[pl.ds(0, 7)], out_send)
    for way in (0, 1):
        for e in (0, 1):
            wait_bytes(whole_amps.at[way, 0, 0], amp_send.at[way, 0, e])
            wait_bytes(whole_amps.at[way, 0, 0, pl.ds(0, ROWS // 2)], amp_send.at[way, 1, e])
            wait_bytes(whole_amps.at[way, 0], amp_send.at[way, 2, e])
            wait_bytes(whole_amps.at[way, 0, pl.ds(0, 2)], amp_send.at[way, 3, e])
    for e in (0, 1):
        wait_bytes(whole_ints.at[0], int_send.at[e])
        wait_bytes(whole_ints.at[0, pl.ds(0, 256)], int_send.at[2 + e])
    wait_bytes(whole_ints.at[pl.ds(0, 4)], sib_send)


def shards(amplitudes, integrals, amp_mask, int_mask, occ_shift, virt_shift):
    amp_gain = jnp.repeat(amp_mask.astype(F32), TILE, axis=1)
    int_gain = jnp.repeat(int_mask.astype(F32), TILE, axis=1)
    dma = pltpu.SemaphoreType.DMA
    vmem, anywhere = pl.BlockSpec(memory_space=pltpu.VMEM), pl.BlockSpec(memory_space=pl.ANY)
    out, _ = pl.pallas_call(
        kernel,
        name="ladder",
        out_shape=(
            jax.ShapeDtypeStruct((8 * ROWS, 128), F32),
            jax.ShapeDtypeStruct((2, 4, 4, ROWS, 128), F32),
        ),
        in_specs=[vmem] * 6,
        out_specs=(anywhere, anywhere),
        scratch_shapes=[
            pltpu.VMEM((2, ROWS, 128), F32),
            pltpu.VMEM((8, 512, COLS), F32),
            pltpu.VMEM((DEPTH, COLS), BF16),
            pltpu.VMEM((DEPTH, COLS), BF16),
            pltpu.VMEM((2, 2, 4, 4, CHUNK, 128), F32),
            pltpu.VMEM((2 * CHUNK, DEPTH), BF16),
            pltpu.VMEM((8, ROWS, 128), F32),
            dma((2, 4, 2)),
            dma((2, 4, 2, CHUNKS)),
            dma((4,)),
            dma((4, PIECES)),
            dma,
            dma((4, PIECES)),
            dma,
            dma((8,)),
            dma((2,)),
            dma((2,)),
        ],
        compiler_params=pltpu.CompilerParams(collective_id=0, has_side_effects=True, vmem_limit_bytes=60 << 20),
        cost_estimate=pl.CostEstimate(flops=6 * ROWS * DEPTH * COLS, bytes_accessed=80 << 20, transcendentals=0),
    )(amplitudes, integrals, amp_gain, int_gain, occ_shift[:, None], virt_shift[None, :])
    return out


def solution(mesh):
    placed = (
        P("row", "col"),
        P("row", "col"),
        P("row", "col"),
        P("row", "col"),
        P("row"),
        P("col"),
    )
    return jax.shard_map(
        shards, mesh=mesh, in_specs=placed, out_specs=P(None, ("col", "row")), check_vma=False
    )
```

time: 546 us -> 219 us (0.40)
  waiting for transfers between devices: 287 us -> 0 us
  Pallas kernels: 0 us -> 208 us
  matrix products: 114 us -> 0 us
  blocking collectives: 102 us -> 0 us
  between operations: 13.4 us -> 0.02 us
  local copies, waits for them, and re-layouts: 21.9 us -> 9.56 us
  other arithmetic: 7.21 us -> 1.37 us
    all_gather x2 -> x0, waiting for transfers between devices: 287 us -> none  [the longest x1 208 us: shards(): lax.all_gather(masked_amps, 'col', axis=1, tiled=True)]
    pallas_call x0 -> x1, Pallas kernels: none -> 208 us  [shards(): pl.pallas_call(kernel, name='ladder', out_shape=(jax.ShapeDtypeStruct((8...]
    dot_general x1 -> x0, matrix products: 114 us -> none  [shards(): jnp.dot(lax.all_gather(masked_amps, 'col', axis=1, tiled=True), whole_int...]
    all_to_all x1 -> x0, blocking collectives: 102 us -> none  [shards(): lax.all_to_all(scaled, 'row', split_axis=1, concat_axis=0, tiled=True)]
    mul x4 -> x0, local copies, waits for them, and re-layouts: 12.7 us -> none  [apply_mask(): tiled = tiled * mask.astype(jnp.float32)[:, None, :, None]]
    all_to_all x1 -> x0, local copies, waits for them, and re-layouts: 9.11 us -> none  [shards(): lax.all_to_all(scaled, 'row', split_axis=1, concat_axis=0, tiled=True)]
    mul x2 -> x0, other arithmetic: 6.51 us -> none  [apply_mask(): tiled = tiled * mask.astype(jnp.float32)[:, None, :, None]]
    unnamed x6 -> x1, local copies, waits for them, and re-layouts: 0.01 us -> 5.86 us
  transfers between devices with their start and end apart: 2 -> 0, of which waited for: 2 -> 0; matrix products, arithmetic and copies ran while one was open for 2% -> 0% of each run, Pallas kernels for 0% -> 0%
where the time goes in v1:
time: 219 us; the launch traced here: 218 us
  Pallas kernels  208 us (95%)
  local copies, waits for them, and re-layouts  9.56 us (4%)
    pallas_call x1, Pallas kernels, shards(): pl.pallas_call(kernel, name='ladder', out_shape=(jax.ShapeDtypeStruct((8...  208 us
    unnamed x1, local copies, waits for them, and re-layouts  5.86 us

profile of v1, /device:TPU:1, one launch (start us, length us, event | category | flops | bytes accessed | tf_op | source)
XLA Modules:
  0.0 218.5 jit_solution(13530248473412478009)
XLA Ops:
  0.0 0.7 convert_element_type.6
  0.7 0.7 convert_element_type.7
  1.4 0.1 copy.8
  1.5 0.1 broadcast_in_dim.12
  1.6 0.7 reshape.6.amp_gain
  2.3 0.1 broadcast_in_dim.13
  2.4 0.7 reshape.7.int_gain
  3.1 2.0 copy.9.occ
  5.1 207.5 %ladder.1 = (f32[16384,128]{1,0:T(8,128)}, f32[2,4,4,2048,128]{4,3,2,1,0:T(8,128)}) custom-call(f32[2048,256]{1,0:T(8,128)} %amps.1, f32[512,1024]{1,0:T(8,128)} %ints.1, f32[32,256]{1,0:T(8,128)} %reshape.6.amp_gain, f32[8,1024]{1,0:T(8,128)} %reshape.7.int_gain, f32[2048,1]{1,0:T(8,128)} %copy.9.occ, f32[1,1024]{1,0:T(1,128)} %bitcast.3), custom_call_target="tpu_custom_call" | custom-call | flops 51539607552 | bytes 83886080 | tf_op jit(solution)/shard_map/ladder/pallas_call | solution.py:301
  212.6 5.9 %copy.11 = f32[16384,128]{1,0:T(8,128)} copy(f32[16384,128]{1,0:T(8,128)} %get-tuple-element.6) | data formatting | bytes 16777216

commit v2 on v1

--- a/solution.py
+++ b/solution.py
@@ -25,7 +25,7 @@
     pltpu.make_async_copy(ref, ref, sem).wait()
 
 
-def kernel(
+def whole_kernel(
     amps, ints, amp_gain, int_gain, occ, virt,
     out, whole_amps,
     own, whole_ints, high, low, chunk_in, split, stage,
@@ -293,14 +293,14 @@
     wait_bytes(whole_ints.at[pl.ds(0, 4)], sib_send)
 
 
-def shards(amplitudes, integrals, amp_mask, int_mask, occ_shift, virt_shift):
+def whole_ladder(amplitudes, integrals, amp_mask, int_mask, occ_shift, virt_shift):
     amp_gain = jnp.repeat(amp_mask.astype(F32), TILE, axis=1)
     int_gain = jnp.repeat(int_mask.astype(F32), TILE, axis=1)
     dma = pltpu.SemaphoreType.DMA
     vmem, anywhere = pl.BlockSpec(memory_space=pltpu.VMEM), pl.BlockSpec(memory_space=pl.ANY)
     out, _ = pl.pallas_call(
-        kernel,
-        name="ladder",
+        whole_kernel,
+        name="whole_ladder",
         out_shape=(
             jax.ShapeDtypeStruct((8 * ROWS, 128), F32),
             jax.ShapeDtypeStruct((2, 4, 4, ROWS, 128), F32),
@@ -326,10 +326,542 @@
             dma((2,)),
             dma((2,)),
         ],
-        compiler_params=pltpu.CompilerParams(collective_id=0, has_side_effects=True, vmem_limit_bytes=60 << 20),
+        compiler_params=pltpu.CompilerParams(collective_id=1, has_side_effects=True, vmem_limit_bytes=60 << 20),
         cost_estimate=pl.CostEstimate(flops=6 * ROWS * DEPTH * COLS, bytes_accessed=80 << 20, transcendentals=0),
     )(amplitudes, integrals, amp_gain, int_gain, occ_shift[:, None], virt_shift[None, :])
     return out
+
+
+MOST = 104
+PAIRS = MOST // 4
+STEPS = 13
+STEP = PAIRS // STEPS
+STEP_TILES = MOST // STEPS
+NEED = (1, 2, 3, 4, 5, 6, 7, 7, 8, 9, 9, 10, 11, 12, 12, 13)
+INT_MOST = 100
+INT_PAIRS = INT_MOST // 2
+INT_PIECES = 5
+INT_PIECE = INT_PAIRS // INT_PIECES
+SLOTS = 4
+START = 5
+
+
+def done_before(c):
+    return jnp.minimum(STEPS, START + (10 * c) // 16)
+
+
+def packed_kernel(
+    amps, ints, tables, listing, occ, virt,
+    out, over, whole_amps, whole_ints,
+    own, own_ints, packed, int_a, int_b, high, low, split_a, split_b, stage, plane, ring, flags, plane_s, ring_s,
+    amp_send, amp_recv, int_send, int_recv, sib_send, sib_recv, tab_send, tab_recv, out_send, out_self, out_recv, local, load,
+    int_load, tab_load,
+):
+    row, col = lax.axis_index("row"), lax.axis_index("col")
+    y, core = row // 2, row % 2
+    z, x = col // 4, col % 4
+
+    def at(dy=0, dz=0, dx=0, dcore=0):
+        r = lax.rem(y + dy, 4) * 2 + lax.rem(core + dcore, 2)
+        return r, lax.rem(z + dz, 4) * 4 + lax.rem(x + dx, 4)
+
+    sibling = at(dcore=1)
+    y_next, y_prev = at(dy=1), at(dy=3)
+    x_near = (at(dx=1), at(dx=3))
+    z_near = (at(dz=1), at(dz=3))
+    first, second = (x_near, z_near), (z_near, x_near)
+    partners = [*x_near, *z_near, sibling] + [at(dy=d, dcore=c) for d in (1, 2, 3) for c in (0, 1)]
+
+    barrier = pltpu.get_barrier_semaphore()
+    for partner in partners:
+        pl.semaphore_signal(barrier, inc=1, device_id=partner, device_id_type=MESH)
+    pl.semaphore_wait(barrier, len(partners))
+
+    def remote(src, dst, send, recv, device):
+        pltpu.make_async_remote_copy(
+            src_ref=src, dst_ref=dst, send_sem=send, recv_sem=recv, device_id=device, device_id_type=MESH
+        ).start()
+
+    def plane_at(dz, dx):
+        return plane.at[lax.rem(z + dz, 4), lax.rem(x + dx, 4)]
+
+    def line_at(dz):
+        return plane.at[lax.rem(z + dz, 4)]
+
+    def ring_at(dy):
+        return ring.at[lax.rem(y + dy, 4)]
+
+    def tab(k, ref, device):
+        remote(ref, ref, tab_send.at[k], tab_recv.at[k], device)
+
+    def tab_wait(k, ref):
+        wait_bytes(ref, tab_recv.at[k])
+
+    def ring0():
+        ring[y, core] = tables[...]
+        tab(6, ring.at[y, core], sibling)
+
+    def ring1():
+        tab_wait(6, ring.at[y, 1 - core])
+        tab(7, ring_at(0), y_next)
+        tab(8, ring_at(0), y_prev)
+
+    def ring2():
+        tab_wait(7, ring_at(3))
+        tab(9, ring_at(3), y_next)
+        tab_wait(8, ring_at(1))
+
+    def ring3():
+        tab_wait(9, ring_at(2))
+        pltpu.make_async_copy(ring, ring_s, tab_load).start()
+        pltpu.make_async_copy(ring, ring_s, tab_load).wait()
+
+    def plane0():
+        plane[z, x] = tables[...]
+        tab(0, plane_at(0, 0), x_near[0])
+        tab(1, plane_at(0, 0), x_near[1])
+
+    def plane1():
+        tab_wait(0, plane_at(0, 3))
+        tab(2, plane_at(0, 3), x_near[0])
+        tab_wait(1, plane_at(0, 1))
+
+    def plane2():
+        tab_wait(2, plane_at(0, 2))
+        tab(3, line_at(0), z_near[0])
+        tab(4, line_at(0), z_near[1])
+
+    def plane3():
+        tab_wait(3, line_at(3))
+        tab(5, line_at(3), z_near[0])
+        tab_wait(4, line_at(1))
+
+    def plane4():
+        tab_wait(5, line_at(2))
+        pltpu.make_async_copy(plane, plane_s, tab_load).start()
+        pltpu.make_async_copy(plane, plane_s, tab_load).wait()
+
+    def flag0():
+        most = jnp.zeros((8, 128), jnp.int32)
+        for zz in range(4):
+            for xx in range(4):
+                most = jnp.maximum(most, plane[zz, xx])
+        flags[y, core] = most
+        tab(10, flags.at[y, core], sibling)
+
+    def flag1():
+        tab_wait(10, flags.at[y, 1 - core])
+        tab(11, flags.at[y], y_next)
+        tab(12, flags.at[y], y_prev)
+
+    def flag2():
+        tab_wait(11, flags.at[lax.rem(y + 3, 4)])
+        tab(13, flags.at[lax.rem(y + 3, 4)], y_next)
+        tab_wait(12, flags.at[lax.rem(y + 1, 4)])
+
+    def flag3():
+        tab_wait(13, flags.at[lax.rem(y + 2, 4)])
+        most = jnp.zeros((8, 128), jnp.int32)
+        for yy in range(4):
+            for cc in range(2):
+                most = jnp.maximum(most, flags[yy, cc])
+        over[...] = most
+
+    def tab_end():
+        for k, ref in enumerate((
+            plane_at(0, 0), plane_at(0, 0), plane_at(0, 0), line_at(0), line_at(0), line_at(0), ring.at[0, 0], ring_at(0),
+            ring_at(0), ring_at(0), flags.at[0, 0], flags.at[0], flags.at[0], flags.at[0],
+        )):
+            wait_bytes(ref, tab_send.at[k])
+
+    lane = lax.broadcasted_iota(jnp.int32, (TILE, 128), 1)
+    lane_row = lax.broadcasted_iota(jnp.int32, (1, 128), 1)
+
+    def beside(left, right, left_kind, right_kind):
+        kinds = jnp.where(lane_row < 64, left_kind, right_kind)
+        straight = (kinds & 1).astype(F32)
+        turned = (kinds >> 1).astype(F32)
+        return (
+            jnp.where(lane < 64, left, right) * straight
+            + pltpu.roll(jnp.where(lane < 64, right, left), 64, 1) * turned
+        )
+
+    def rows_of(c, part=None):
+        return pl.ds(c * STEP, STEP) if part is None else pl.ds(c * STEP + part, 1)
+
+    def block(way, dz, dx, rows):
+        return whole_amps.at[way, lax.rem(z + dz, 4), lax.rem(x + dx, 4), rows]
+
+    def bundle(way, d, rows):
+        if way == 0:
+            return whole_amps.at[0, lax.rem(z + d, 4), :, rows]
+        return whole_amps.at[1, :, lax.rem(x + d, 4), rows]
+
+    def near(way, d, rows):
+        return block(way, 0, d, rows) if way == 0 else block(way, d, 0, rows)
+
+    def step1(c):
+        rows = rows_of(c)
+        for way in (0, 1):
+            for e in (0, 1):
+                remote(own.at[way, rows], block(way, 0, 0, rows), amp_send.at[way, 0, e], amp_recv.at[way, 0, e, c], first[way][e])
+
+    def step2(c):
+        for way in (0, 1):
+            for e in (0, 1):
+                d = 3 if e == 0 else 1
+                wait_bytes(near(way, d, rows_of(c)), amp_recv.at[way, 0, e, c])
+                part = near(way, d, rows_of(c, e))
+                remote(part, part, amp_send.at[way, 1, e], amp_recv.at[way, 1, e, c], first[way][e])
+
+    def step3(c):
+        for way in (0, 1):
+            for e in (0, 1):
+                wait_bytes(near(way, 2, rows_of(c, e)), amp_recv.at[way, 1, e, c])
+            line = bundle(way, 0, rows_of(c))
+            for e in (0, 1):
+                remote(line, line, amp_send.at[way, 2, e], amp_recv.at[way, 2, e, c], second[way][e])
+
+    def step4(c):
+        for way in (0, 1):
+            for e in (0, 1):
+                d = 3 if e == 0 else 1
+                wait_bytes(bundle(way, d, rows_of(c)), amp_recv.at[way, 2, e, c])
+                part = bundle(way, d, rows_of(c, e))
+                remote(part, part, amp_send.at[way, 3, e], amp_recv.at[way, 3, e, c], second[way][e])
+
+    def step5(c):
+        for way in (0, 1):
+            for e in (0, 1):
+                wait_bytes(bundle(way, 2, rows_of(c, e)), amp_recv.at[way, 3, e, c])
+
+    def tick(t):
+        for lead, step in ((8, step1), (6, step2), (4, step3), (2, step4), (0, step5)):
+            c = t + lead
+            pl.when((c >= (8 if lead == 8 else 0)) & (c < STEPS))(functools.partial(step, c))
+
+    def fetch(s):
+        rows = rows_of(s)
+        return pltpu.make_async_copy(whole_amps.at[:, :, :, rows], packed.at[:, :, :, rows], load)
+
+    def int_rows(p, part=None):
+        half = INT_PIECE // 2
+        return pl.ds(p * INT_PIECE, INT_PIECE) if part is None else pl.ds(p * INT_PIECE + part * half, half)
+
+    def int_block(dy, dcore, rows):
+        return whole_ints.at[lax.rem(y + dy, 4) * 2 + lax.rem(core + dcore, 2), rows]
+
+    def unpack_ints(ref, dy, dcore):
+        yy, cc = lax.rem(y + dy, 4), lax.rem(core + dcore, 2)
+
+        @pl.loop(0, 8)
+        def _(t):
+            rows = pl.ds(pl.multiple_of((yy * 2 + cc) * 512 + t * TILE, TILE), TILE)
+            for g in range(8):
+                one = t * 16 + 2 * g
+                two = one + 1
+                value = beside(
+                    ref[ring_s[yy, cc, 3, one]], ref[ring_s[yy, cc, 3, two]], ring_s[yy, cc, 4, one], ring_s[yy, cc, 4, two]
+                )
+                top = value.astype(BF16)
+                high[rows, g * 128:(g + 1) * 128] = top
+                low[rows, g * 128:(g + 1) * 128] = (value - top.astype(F32)).astype(BF16)
+
+    def int_start(p):
+        rows = int_rows(p)
+        piece, there = own_ints.at[rows], int_block(0, 0, rows)
+        remote(piece, there, int_send.at[0], int_recv.at[0, p], y_next)
+        remote(piece, there, int_send.at[1], int_recv.at[1, p], y_prev)
+
+    def int_pass(p):
+        rows = int_rows(p)
+        for e, d, device in ((0, 3, y_next), (1, 1, y_prev)):
+            piece = int_block(d, 0, rows)
+            wait_bytes(piece, int_recv.at[e, p])
+            part = int_block(d, 0, int_rows(p, e))
+            remote(part, part, int_send.at[2 + e], int_recv.at[2 + e, p], device)
+            remote(piece, piece, sib_send, sib_recv.at[1 + e, p], sibling)
+
+    def int_in(k, buffer, dy, dcore):
+        if dcore:
+            if k == 0:
+                wait_bytes(int_block(0, 1, pl.ds(0, INT_PAIRS)), sib_recv.at[0, 0])
+            else:
+                @pl.loop(0, INT_PIECES)
+                def _(p):
+                    wait_bytes(int_block(dy, 1, int_rows(p)), sib_recv.at[k, p])
+        copy = pltpu.make_async_copy(int_block(dy, dcore, pl.ds(0, INT_PAIRS)), buffer, int_load.at[0 if buffer is int_a else 1])
+        copy.start()
+        return copy
+
+    def int_far(p):
+        for e in (0, 1):
+            wait_bytes(int_block(2, 0, int_rows(p, e)), int_recv.at[2 + e, p])
+        piece = int_block(2, 0, int_rows(p))
+        remote(piece, piece, sib_send, sib_recv.at[3, p], sibling)
+
+    ring0()
+    plane0()
+
+    @pl.loop(0, PAIRS)
+    def _(i):
+        for way in (0, 1):
+            pair = 2 * i + way
+            tiles = []
+            for place in (2 * pair, 2 * pair + 1):
+                both = amps[listing[0, place]]
+                tiles.append(both[:, :128] * listing[1, place].astype(F32) + both[:, 128:] * listing[2, place].astype(F32))
+            own[way, i] = beside(*tiles, listing[3, 2 * pair], listing[3, 2 * pair + 1])
+
+    for c in range(8):
+        step1(c)
+    ring1()
+
+    for t in range(8):
+        for g in range(8):
+            stage[t // 2, g, t % 2] = ints[t * TILE:(t + 1) * TILE, g * 128:(g + 1) * 128]
+
+    @pl.loop(0, INT_PAIRS)
+    def _(pair):
+        one = 2 * pair
+        two = one + 1
+        own_ints[pair] = beside(
+            stage[listing[4, one], listing[5, one], listing[6, one]], stage[listing[4, two], listing[5, two], listing[6, two]],
+            listing[7, one], listing[7, two],
+        )
+
+    ring2()
+
+    @pl.loop(0, INT_PIECES)
+    def _(p):
+        int_start(p)
+
+    remote(own_ints, int_block(0, 0, pl.ds(0, INT_PAIRS)), sib_send, sib_recv.at[0, 0], sibling)
+    for way in (0, 1):
+        pltpu.make_async_copy(own.at[way], whole_amps.at[way, z, x], local.at[way]).start()
+    for way in (0, 1):
+        pltpu.make_async_copy(own.at[way], whole_amps.at[way, z, x], local.at[way]).wait()
+
+    tick(-6)
+    plane1()
+    tick(-5)
+    tick(-4)
+    plane2()
+    tick(-3)
+    ring3()
+    tick(-2)
+    unpack_ints(own_ints, 0, 0)
+    plane3()
+    tick(-1)
+    other = int_in(0, int_a, 0, 1)
+    tick(0)
+    plane4()
+    int_pass(0)
+    flag0()
+    other.wait()
+    unpack_ints(int_a, 0, 1)
+    int_pass(1)
+    tick(1)
+    flag1()
+    int_pass(2)
+    tick(2)
+    int_pass(3)
+    tick(3)
+    int_pass(4)
+    left, right = int_in(None, int_a, 3, 0), int_in(None, int_b, 1, 0)
+    left.wait()
+    unpack_ints(int_a, 3, 0)
+    left = int_in(1, int_a, 3, 1)
+    right.wait()
+    unpack_ints(int_b, 1, 0)
+    right = int_in(2, int_b, 1, 1)
+    flag2()
+    left.wait()
+    unpack_ints(int_a, 3, 1)
+    right.wait()
+    unpack_ints(int_b, 1, 1)
+    tick(4)
+
+    @pl.loop(0, START)
+    def _(s):
+        fetch(s).start()
+
+    @pl.loop(0, INT_PIECES)
+    def _(p):
+        int_far(p)
+
+    left = int_in(None, int_a, 2, 0)
+    wait_bytes(whole_amps.at[:, :, :, pl.ds(0, START * STEP)], load)
+    left.wait()
+    unpack_ints(int_a, 2, 0)
+    right = int_in(3, int_b, 2, 1)
+    right.wait()
+    unpack_ints(int_b, 2, 1)
+
+    def stage_wait(slot):
+        wait_bytes(stage.at[slot, pl.ds(0, 7)], out_send.at[slot])
+        wait_bytes(stage.at[slot, 0], out_self.at[slot])
+
+    def unpack_amps(split, c, zz, xx, at_k):
+        for t in (0, 1):
+            for g in (0, 1):
+                one = (c * 2 + t) * 4 + 2 * g
+                two = one + 1
+                value = beside(
+                    packed[plane_s[zz, xx, 0, one], zz, xx, plane_s[zz, xx, 1, one]],
+                    packed[plane_s[zz, xx, 0, two], zz, xx, plane_s[zz, xx, 1, two]],
+                    plane_s[zz, xx, 2, one], plane_s[zz, xx, 2, two],
+                )
+                top = value.astype(BF16)
+                lanes = pl.ds(pl.multiple_of(at_k + g * 128, 128), 128)
+                split[t * TILE:(t + 1) * TILE, lanes] = top
+                split[CHUNK + t * TILE:CHUNK + (t + 1) * TILE, lanes] = (value - top.astype(F32)).astype(BF16)
+
+    @pl.loop(0, 16)
+    def _(k):
+        unpack_amps(split_a, 0, k // 4, lax.rem(k, 4), k * 256)
+
+    def multiply(c, split, split_next):
+        before, after = done_before(c), done_before(c + 1)
+
+        @pl.when(after > before)
+        def _():
+            tick(after - 1)
+
+        slot = lax.rem(c, SLOTS)
+        pl.when(c >= SLOTS)(functools.partial(stage_wait, slot))
+        shift = jnp.transpose(jnp.broadcast_to(occ[pl.ds(c, 1), :], (CHUNK, 128)))
+        later = jnp.minimum(c + 1, CHUNKS - 1)
+
+        @pl.loop(0, COLS // WIDE)
+        def _(n):
+            wide = pl.ds(pl.multiple_of(n * WIDE, WIDE), WIDE)
+            both = jnp.dot(split[...], high[:, wide], preferred_element_type=F32)
+            for k in range(8):
+                unpack_amps(split_next, later, n * 2 + k // 4, k % 4, n * 2048 + k * 256)
+            rest = jnp.dot(split[0:CHUNK], low[:, wide], preferred_element_type=F32)
+            ladder = both[:CHUNK] + (both[CHUNK:] + rest)
+            for q in range(WIDE // 128):
+                at_q = n * (WIDE // 128) + q
+                scaled = ladder[:, q * 128:(q + 1) * 128] / (shift + virt[pl.ds(at_q, 1), :])
+                stage[slot, at_q, 0] = scaled[:TILE]
+                stage[slot, at_q, 1] = scaled[TILE:]
+
+        there = pl.ds(row * (ROWS // TILE) + c * (CHUNK // TILE), CHUNK // TILE)
+        for d in (4, 5, 2, 3, 6, 7, 1):
+            owner = lax.rem(row + d, 8)
+            remote(stage.at[slot, owner], out.at[there], out_send.at[slot], out_recv.at[row], (owner, col))
+        pltpu.make_async_copy(stage.at[slot, row], out.at[there], out_self.at[slot]).start()
+
+        @pl.when(after > before)
+        def _():
+            fetch(after - 1).start()
+            fetch(after - 1).wait()
+
+    @pl.loop(0, CHUNKS // 2)
+    def _(i):
+        multiply(2 * i, split_a, split_b)
+        multiply(2 * i + 1, split_b, split_a)
+
+    flag3()
+    for slot in range(SLOTS):
+        stage_wait(slot)
+    for d in range(1, 8):
+        source = lax.rem(row + d, 8)
+        wait_bytes(out.at[pl.ds(source * (ROWS // TILE), ROWS // TILE)], out_recv.at[source])
+    for way in (0, 1):
+        for e in (0, 1):
+            wait_bytes(whole_amps.at[way, 0, 0], amp_send.at[way, 0, e])
+            wait_bytes(whole_amps.at[way, 0, 0, pl.ds(0, PAIRS // 2)], amp_send.at[way, 1, e])
+            wait_bytes(whole_amps.at[way, 0], amp_send.at[way, 2, e])
+            wait_bytes(whole_amps.at[way, 0, pl.ds(0, 2)], amp_send.at[way, 3, e])
+    for e in (0, 1):
+        wait_bytes(whole_ints.at[0], int_send.at[e])
+        wait_bytes(whole_ints.at[0, pl.ds(0, INT_PAIRS // 2)], int_send.at[2 + e])
+    wait_bytes(whole_ints.at[pl.ds(0, 4)], sib_send)
+    tab_end()
+
+
+def packed_ladder(amplitudes, integrals, tables, listing, occ_shift, virt_shift):
+    dma = pltpu.SemaphoreType.DMA
+    vmem, anywhere = pl.BlockSpec(memory_space=pltpu.VMEM), pl.BlockSpec(memory_space=pl.ANY)
+    out, over, _, _ = pl.pallas_call(
+        packed_kernel,
+        name="packed_ladder",
+        out_shape=(
+            jax.ShapeDtypeStruct((8 * ROWS // TILE, TILE, 128), F32),
+            jax.ShapeDtypeStruct((8, 128), jnp.int32),
+            jax.ShapeDtypeStruct((2, 4, 4, PAIRS, TILE, 128), F32),
+            jax.ShapeDtypeStruct((8, INT_PAIRS, TILE, 128), F32),
+        ),
+        in_specs=[vmem] * 3 + [pl.BlockSpec(memory_space=pltpu.SMEM)] + [vmem] * 2,
+        out_specs=(anywhere, vmem, anywhere, anywhere),
+        scratch_shapes=[
+            pltpu.VMEM((2, PAIRS, TILE, 128), F32),
+            pltpu.VMEM((INT_PAIRS, TILE, 128), F32),
+            pltpu.VMEM((2, 4, 4, PAIRS, TILE, 128), F32),
+            pltpu.VMEM((INT_PAIRS, TILE, 128), F32),
+            pltpu.VMEM((INT_PAIRS, TILE, 128), F32),
+            pltpu.VMEM((DEPTH, COLS), BF16),
+            pltpu.VMEM((DEPTH, COLS), BF16),
+            pltpu.VMEM((2 * CHUNK, DEPTH), BF16),
+            pltpu.VMEM((2 * CHUNK, DEPTH), BF16),
+            pltpu.VMEM((SLOTS, 8, CHUNK // TILE, TILE, 128), F32),
+            pltpu.VMEM((4, 4, 8, 128), jnp.int32),
+            pltpu.VMEM((4, 2, 8, 128), jnp.int32),
+            pltpu.VMEM((4, 2, 8, 128), jnp.int32),
+            pltpu.SMEM((4, 4, 8, 128), jnp.int32),
+            pltpu.SMEM((4, 2, 8, 128), jnp.int32),
+            dma((2, 4, 2)),
+            dma((2, 4, 2, STEPS)),
+            dma((4,)),
+            dma((4, INT_PIECES)),
+            dma,
+            dma((4, INT_PIECES)),
+            dma((14,)),
+            dma((14,)),
+            dma((SLOTS,)),
+            dma((SLOTS,)),
+            dma((8,)),
+            dma((2,)),
+            dma,
+            dma((2,)),
+            dma,
+        ],
+        compiler_params=pltpu.CompilerParams(collective_id=0, has_side_effects=True, vmem_limit_bytes=61 << 20),
+        cost_estimate=pl.CostEstimate(flops=6 * ROWS * DEPTH * COLS, bytes_accessed=80 << 20, transcendentals=0),
+    )(
+        amplitudes.reshape(ROWS // TILE, TILE, 256), integrals, tables, listing, occ_shift.reshape(CHUNKS, 128),
+        virt_shift.reshape(8, 128),
+    )
+    return out.reshape(8 * ROWS, 128), over[5, 0]
+
+
+def shards(amplitudes, integrals, amp_mask, int_mask, occ_shift, virt_shift):
+    masks = jnp.stack([amp_mask.reshape(128), int_mask.reshape(128)])
+    count = jnp.arange(128, dtype=jnp.int32)
+    slots = jnp.sum(jnp.where(count[:, None] < count[None, :], masks[:, :, None], 0), axis=1)
+    used = slots + masks
+    room = jnp.array([STEP_TILES * n for n in NEED], jnp.int32)
+    over = jnp.any(used[0].reshape(CHUNKS, 8)[:, 7] > room) | (used[1, 127] > INT_MOST)
+    limit = jnp.array([[MOST - 1], [INT_MOST - 1]], jnp.int32)
+    at = jnp.where(masks != 0, jnp.minimum(slots, limit), 0)
+    kind = jnp.where(masks != 0, 1 + ((at ^ count[None, :]) & 1), 0)
+    here = (masks[:, :, None] != 0) & (slots[:, :, None] == count[None, None, :])
+    place = jnp.sum(jnp.where(here, count[None, :, None], 0), axis=1)
+    turn = 1 + ((place ^ count[None, :]) & 1)
+    flags = jnp.broadcast_to(over.astype(jnp.int32), (128,))
+    tables = jnp.stack([(at[0] >> 1) & 1, at[0] >> 2, kind[0], at[1] >> 1, kind[1], flags, flags, flags])
+    a, b = place
+    listing = jnp.stack([
+        a >> 2, 1 - ((a >> 1) & 1), (a >> 1) & 1, turn[0], b >> 5, (b >> 1) & 7, (b >> 4) & 1, turn[1]
+    ])
+    update, over = packed_ladder(amplitudes, integrals, tables, listing, occ_shift, virt_shift)
+    return lax.cond(
+        over > 0,
+        lambda: whole_ladder(amplitudes, integrals, amp_mask, int_mask, occ_shift, virt_shift),
+        lambda: update,
+    )
 
 
 def solution(mesh):

time: 219 us -> 219 us (level)
  Pallas kernels: 208 us -> 202 us
    pallas_call x1, Pallas kernels: 208 us -> 202 us  [packed_ladder(): pl.pallas_call(packed_kernel, name='packed_ladder', out_shape=(jax.ShapeD...]
    broadcast_in_dim x3 -> x0, local copies, waits for them, and re-layouts: 2.19 us -> none  [the longest x1 2.04 us: shards(): occ_shift[:, None]]
    unnamed x1 -> x12, local copies, waits for them, and re-layouts: 5.86 us -> 6.64 us
where the time goes in v2:
time: 219 us; the launch traced here: 218 us
  Pallas kernels  202 us (92%)
  local copies, waits for them, and re-layouts  10.6 us (5%)
  other arithmetic  3.19 us (1%)
    pallas_call x1, Pallas kernels, packed_ladder(): pl.pallas_call(packed_kernel, name='packed_ladder', out_shape=(jax.ShapeD...  202 us
    unnamed x12, local copies, waits for them, and re-layouts  6.64 us

profile of v2, /device:TPU:1, one launch (start us, length us, event | category | flops | bytes accessed | tf_op | source)
XLA Modules:
  0.0 218.1 jit_solution(4825102688696253326)
XLA Ops:
  0.0 0.8 stack_reshape.7
  0.8 0.8 copy.17
  1.5 0.1 stack_reshape.6
  1.7 0.1 select_reduce_fusion.1
  1.8 0.7 add_select_fusion
  2.5 0.6 slice.37
  3.8 0.1 select_reduce_fusion
  3.9 0.7 minimum_select_fusion
  4.7 0.6 stack.8.listing
  5.3 0.1 reshape_squeeze.3
  5.4 1.4 fusion.1
  7.5 0.6 stack.7.tables
  8.1 0.0 copy-start
  8.1 0.0 copy-start.1
  8.1 0.0 copy-start.2
  8.1 0.0 copy-start.3
  8.1 0.0 copy-start.4
  8.1 202.1 %packed_ladder.1 = (f32[256,64,128]{2,1,0:T(8,128)}, s32[8,128]{1,0:T(8,128)}, f32[2,4,4,26,64,128]{5,4,3,2,1,0:T(8,128)}, f32[8,50,64,128]{3,2,1,0:T(8,128)}) custom-call(f32[32,64,256]{2,1,0:T(8,128)} %bitcast.11, f32[512,1024]{1,0:T(8,128)} %ints.1, s32[8,128]{1,0:T(8,128)} %stack.7.tables, s32[8,128]{1,0:T(8,128)} %stack.8.listing, f32[16,128]{1,0:T(8,128)} %bitcast.9, ...), custom_call_target="tpu_custom_call" | custom-call | flops 51539607552 | bytes 83886080 | tf_op jit(solution)/shard_map/packed_ladder/pallas_call | solution.py:788
  210.2 1.2 slice.40
  212.0 0.0 copy-done
  212.0 0.0 copy-done.1
  212.0 0.0 copy-done.2
  212.1 0.0 copy-done.3
  212.1 0.0 copy-done.4
  212.1 0.2 conditional.1
  212.3 5.9 %copy.23 = f32[16384,128]{1,0:T(8,128)} copy(f32[16384,128]{1,0:T(8,128)} %get-tuple-element.34) | data formatting | bytes 16777216
  (7 shorter events, 0.1 us)
Async XLA Ops:
  8.1 203.9 %copy-start = (s32[8,16]{1,0:T(8,128)S(1)}, s32[8,16]{1,0:T(8,128)}, u32[]{:S(2)}) copy-start(s32[8,16]{1,0:T(8,128)} %param.13) | copy-start | bytes 1540
  8.1 204.0 %copy-start.1 = (f32[2048]{0:T(1024)S(1)}, f32[2048]{0:T(1024)}, u32[]{:S(2)}) copy-start(f32[2048]{0:T(1024)} %param.14) | copy-start | bytes 24580
  8.1 204.0 %copy-start.2 = (s32[32,4]{0,1:T(4,128)S(1)}, s32[32,4]{0,1:T(4,128)}, u32[]{:S(2)}) copy-start(s32[32,4]{0,1:T(4,128)} %param.12) | copy-start | bytes 1540
  8.1 204.0 %copy-start.3 = (f32[2048,256]{1,0:T(8,128)S(1)}, f32[2048,256]{1,0:T(8,128)}, u32[]{:S(2)}) copy-start(f32[2048,256]{1,0:T(8,128)} %param.10) | copy-start | bytes 6291460
  8.1 204.0 %copy-start.4 = (f32[1024]{0:T(1024)S(1)}, f32[1024]{0:T(1024)}, u32[]{:S(2)}) copy-start(f32[1024]{0:T(1024)} %param.15) | copy-start | bytes 12292

commit v3 on v2

--- a/solution.py
+++ b/solution.py
@@ -338,16 +338,13 @@
 STEP = PAIRS // STEPS
 STEP_TILES = MOST // STEPS
 NEED = (1, 2, 3, 4, 5, 6, 7, 7, 8, 9, 9, 10, 11, 12, 12, 13)
-INT_MOST = 100
+INT_MOST = 104
 INT_PAIRS = INT_MOST // 2
-INT_PIECES = 5
+INT_PIECES = 13
 INT_PIECE = INT_PAIRS // INT_PIECES
-SLOTS = 4
-START = 5
-
-
-def done_before(c):
-    return jnp.minimum(STEPS, START + (10 * c) // 16)
+INT_EARLY = 7
+SLOTS = 8
+EARLY = 6
 
 
 def packed_kernel(
@@ -536,7 +533,7 @@
                 wait_bytes(bundle(way, 2, rows_of(c, e)), amp_recv.at[way, 3, e, c])
 
     def tick(t):
-        for lead, step in ((8, step1), (6, step2), (4, step3), (2, step4), (0, step5)):
+        for lead, step in ((8, step1), (6, step2), (4, step3), (2, step4)):
             c = t + lead
             pl.when((c >= (8 if lead == 8 else 0)) & (c < STEPS))(functools.partial(step, c))
 
@@ -544,6 +541,11 @@
         rows = rows_of(s)
         return pltpu.make_async_copy(whole_amps.at[:, :, :, rows], packed.at[:, :, :, rows], load)
 
+    def arrive(s):
+        step5(s)
+        fetch(s).start()
+        fetch(s).wait()
+
     def int_rows(p, part=None):
         half = INT_PIECE // 2
         return pl.ds(p * INT_PIECE, INT_PIECE) if part is None else pl.ds(p * INT_PIECE + part * half, half)
@@ -551,21 +553,22 @@
     def int_block(dy, dcore, rows):
         return whole_ints.at[lax.rem(y + dy, 4) * 2 + lax.rem(core + dcore, 2), rows]
 
-    def unpack_ints(ref, dy, dcore):
+    def unpack_ints(ref, dy, dcore, half):
         yy, cc = lax.rem(y + dy, 4), lax.rem(core + dcore, 2)
 
         @pl.loop(0, 8)
         def _(t):
             rows = pl.ds(pl.multiple_of((yy * 2 + cc) * 512 + t * TILE, TILE), TILE)
-            for g in range(8):
-                one = t * 16 + 2 * g
+            for g in range(4):
+                one = half * 64 + t * 8 + 2 * g
                 two = one + 1
                 value = beside(
                     ref[ring_s[yy, cc, 3, one]], ref[ring_s[yy, cc, 3, two]], ring_s[yy, cc, 4, one], ring_s[yy, cc, 4, two]
                 )
                 top = value.astype(BF16)
-                high[rows, g * 128:(g + 1) * 128] = top
-                low[rows, g * 128:(g + 1) * 128] = (value - top.astype(F32)).astype(BF16)
+                lanes = slice((half * 4 + g) * 128, (half * 4 + g + 1) * 128)
+                high[rows, lanes] = top
+                low[rows, lanes] = (value - top.astype(F32)).astype(BF16)
 
     def int_start(p):
         rows = int_rows(p)
@@ -582,17 +585,30 @@
             remote(part, part, int_send.at[2 + e], int_recv.at[2 + e, p], device)
             remote(piece, piece, sib_send, sib_recv.at[1 + e, p], sibling)
 
-    def int_in(k, buffer, dy, dcore):
-        if dcore:
-            if k == 0:
+    def int_take(blocks, half):
+        first, last = ((0, INT_EARLY), (INT_EARLY, INT_PIECES))[half]
+
+        def enter(i):
+            k, dy, dcore = blocks[i]
+            if dcore and k == 0:
                 wait_bytes(int_block(0, 1, pl.ds(0, INT_PAIRS)), sib_recv.at[0, 0])
-            else:
-                @pl.loop(0, INT_PIECES)
+            elif dcore:
+                @pl.loop(first, last)
                 def _(p):
                     wait_bytes(int_block(dy, 1, int_rows(p)), sib_recv.at[k, p])
-        copy = pltpu.make_async_copy(int_block(dy, dcore, pl.ds(0, INT_PAIRS)), buffer, int_load.at[0 if buffer is int_a else 1])
-        copy.start()
-        return copy
+            pairs = pl.ds(0, INT_PAIRS if half or k == 0 else INT_EARLY * INT_PIECE)
+            buffer = (int_a, int_b)[i % 2]
+            copy = pltpu.make_async_copy(int_block(dy, dcore, pairs), buffer.at[pairs], int_load.at[i % 2])
+            copy.start()
+            return copy
+
+        copy = enter(0)
+        for i, (k, dy, dcore) in enumerate(blocks):
+            copy.wait()
+            copy = enter(i + 1) if i + 1 < len(blocks) else None
+            unpack_ints((int_a, int_b)[i % 2], dy, dcore, half)
+            if k == 0:
+                unpack_ints((int_a, int_b)[i % 2], dy, dcore, 1)
 
     def int_far(p):
         for e in (0, 1):
@@ -619,7 +635,7 @@
 
     for t in range(8):
         for g in range(8):
-            stage[t // 2, g, t % 2] = ints[t * TILE:(t + 1) * TILE, g * 128:(g + 1) * 128]
+            stage[t, g // 2, g % 2] = ints[t * TILE:(t + 1) * TILE, g * 128:(g + 1) * 128]
 
     @pl.loop(0, INT_PAIRS)
     def _(pair):
@@ -632,7 +648,7 @@
 
     ring2()
 
-    @pl.loop(0, INT_PIECES)
+    @pl.loop(0, INT_EARLY)
     def _(p):
         int_start(p)
 
@@ -650,56 +666,46 @@
     tick(-3)
     ring3()
     tick(-2)
-    unpack_ints(own_ints, 0, 0)
+    unpack_ints(own_ints, 0, 0, 0)
+    unpack_ints(own_ints, 0, 0, 1)
     plane3()
+    for p in range(2):
+        int_pass(p)
     tick(-1)
-    other = int_in(0, int_a, 0, 1)
+    int_take([(0, 0, 1)], 0)
+    plane4()
+    flag0()
+
+    @pl.loop(2, INT_EARLY)
+    def _(p):
+        int_pass(p)
+
+    @pl.loop(INT_EARLY, INT_PIECES)
+    def _(p):
+        int_start(p)
+
     tick(0)
-    plane4()
-    int_pass(0)
-    flag0()
-    other.wait()
-    unpack_ints(int_a, 0, 1)
-    int_pass(1)
+    flag1()
+    int_take([(1, 3, 0), (2, 1, 0), (1, 3, 1), (2, 1, 1)], 0)
     tick(1)
-    flag1()
-    int_pass(2)
-    tick(2)
-    int_pass(3)
-    tick(3)
-    int_pass(4)
-    left, right = int_in(None, int_a, 3, 0), int_in(None, int_b, 1, 0)
-    left.wait()
-    unpack_ints(int_a, 3, 0)
-    left = int_in(1, int_a, 3, 1)
-    right.wait()
-    unpack_ints(int_b, 1, 0)
-    right = int_in(2, int_b, 1, 1)
-    flag2()
-    left.wait()
-    unpack_ints(int_a, 3, 1)
-    right.wait()
-    unpack_ints(int_b, 1, 1)
-    tick(4)
-
-    @pl.loop(0, START)
-    def _(s):
-        fetch(s).start()
-
-    @pl.loop(0, INT_PIECES)
+
+    @pl.loop(0, INT_EARLY)
     def _(p):
         int_far(p)
 
-    left = int_in(None, int_a, 2, 0)
-    wait_bytes(whole_amps.at[:, :, :, pl.ds(0, START * STEP)], load)
-    left.wait()
-    unpack_ints(int_a, 2, 0)
-    right = int_in(3, int_b, 2, 1)
-    right.wait()
-    unpack_ints(int_b, 2, 1)
+    int_take([(3, 2, 0), (3, 2, 1)], 0)
+    tick(2)
+    arrive(0)
+    arrive(1)
+
+    @pl.loop(INT_EARLY, INT_EARLY + 3)
+    def _(p):
+        int_pass(p)
+
+    tick(3)
 
     def stage_wait(slot):
-        wait_bytes(stage.at[slot, pl.ds(0, 7)], out_send.at[slot])
+        wait_bytes(stage.at[slot, pl.ds(0, 3)], out_send.at[slot])
         wait_bytes(stage.at[slot, 0], out_self.at[slot])
 
     def unpack_amps(split, c, zz, xx, at_k):
@@ -721,47 +727,107 @@
     def _(k):
         unpack_amps(split_a, 0, k // 4, lax.rem(k, 4), k * 256)
 
-    def multiply(c, split, split_next):
-        before, after = done_before(c), done_before(c + 1)
-
-        @pl.when(after > before)
+    def multiply(unit, c, n, split, split_next, later, parts):
+        slot = lax.rem(unit, SLOTS)
+        pl.when(unit >= SLOTS)(functools.partial(stage_wait, slot))
+        shift = jnp.transpose(jnp.broadcast_to(occ[pl.ds(c, 1), :], (CHUNK, 128)))
+        wide = pl.ds(pl.multiple_of(n * WIDE, WIDE), WIDE)
+        both = jnp.dot(split[...], high[:, wide], preferred_element_type=F32)
+        for zz, xx, at_k in parts:
+            unpack_amps(split_next, later, zz, xx, at_k)
+        rest = jnp.dot(split[0:CHUNK], low[:, wide], preferred_element_type=F32)
+        ladder = both[:CHUNK] + (both[CHUNK:] + rest)
+        for q in range(4):
+            scaled = ladder[:, q * 128:(q + 1) * 128] / (shift + virt[pl.ds(2 * q + n, 1), :])
+            stage[slot, q, 0] = scaled[:TILE]
+            stage[slot, q, 1] = scaled[TILE:]
+
+        there = pl.ds(row * (ROWS // TILE) + c * (CHUNK // TILE), CHUNK // TILE)
+        for d in (2, 1, 3):
+            owner = lax.rem(y + d, 4)
+            remote(stage.at[slot, owner], out.at[there], out_send.at[slot], out_recv.at[row], (owner * 2 + n, col))
+
+        @pl.when(core == n)
         def _():
-            tick(after - 1)
-
-        slot = lax.rem(c, SLOTS)
-        pl.when(c >= SLOTS)(functools.partial(stage_wait, slot))
-        shift = jnp.transpose(jnp.broadcast_to(occ[pl.ds(c, 1), :], (CHUNK, 128)))
-        later = jnp.minimum(c + 1, CHUNKS - 1)
-
-        @pl.loop(0, COLS // WIDE)
-        def _(n):
-            wide = pl.ds(pl.multiple_of(n * WIDE, WIDE), WIDE)
-            both = jnp.dot(split[...], high[:, wide], preferred_element_type=F32)
-            for k in range(8):
-                unpack_amps(split_next, later, n * 2 + k // 4, k % 4, n * 2048 + k * 256)
-            rest = jnp.dot(split[0:CHUNK], low[:, wide], preferred_element_type=F32)
-            ladder = both[:CHUNK] + (both[CHUNK:] + rest)
-            for q in range(WIDE // 128):
-                at_q = n * (WIDE // 128) + q
-                scaled = ladder[:, q * 128:(q + 1) * 128] / (shift + virt[pl.ds(at_q, 1), :])
-                stage[slot, at_q, 0] = scaled[:TILE]
-                stage[slot, at_q, 1] = scaled[TILE:]
-
-        there = pl.ds(row * (ROWS // TILE) + c * (CHUNK // TILE), CHUNK // TILE)
-        for d in (4, 5, 2, 3, 6, 7, 1):
-            owner = lax.rem(row + d, 8)
-            remote(stage.at[slot, owner], out.at[there], out_send.at[slot], out_recv.at[row], (owner, col))
-        pltpu.make_async_copy(stage.at[slot, row], out.at[there], out_self.at[slot]).start()
-
-        @pl.when(after > before)
+            pltpu.make_async_copy(stage.at[slot, y], out.at[there], out_self.at[slot]).start()
+
+        @pl.when(core != n)
         def _():
-            fetch(after - 1).start()
-            fetch(after - 1).wait()
-
-    @pl.loop(0, CHUNKS // 2)
+            remote(stage.at[slot, y], out.at[there], out_self.at[slot], out_recv.at[row], sibling)
+
+    def after(value, points):
+        return sum((value >= p).astype(jnp.int32) for p in points)
+
+    def among(value, points):
+        return functools.reduce(lambda a, b: a | b, [value == p for p in points])
+
+    @pl.loop(0, 16)
+    def _(k):
+        unpack_amps(split_a, 0, k // 4, lax.rem(k, 4), k * 256)
+
+    everything = [(k // 4, k % 4, k * 256) for k in range(16)]
+
+    @pl.loop(0, EARLY)
     def _(i):
-        multiply(2 * i, split_a, split_b)
-        multiply(2 * i + 1, split_b, split_a)
+        for odd, split, split_next in ((0, split_a, split_b), (1, split_b, split_a)):
+            unit = 2 * i + odd
+            n = unit // EARLY
+            c = unit - n * EARLY
+
+            @pl.when(among(unit, (3, 4, 7, 10)))
+            def _():
+                tick(4 + after(unit, (4, 7, 10)))
+
+            @pl.when(among(unit, (1, 2, 3, 4, 11)))
+            def _():
+                arrive(jnp.where(unit == 11, 6, unit + 1))
+
+            later = jnp.where((unit == EARLY - 1), 0, c + 1)
+            multiply(unit, c, n, split, split_next, later, everything)
+            if odd == 0:
+                @pl.when(i == 0)
+                def _():
+                    int_pass(INT_EARLY + 3)
+                    int_pass(INT_EARLY + 4)
+
+                @pl.when(i == 2)
+                def _():
+                    @pl.loop(INT_EARLY, INT_PIECES)
+                    def _(p):
+                        int_far(p)
+            else:
+                @pl.when(i == 0)
+                def _():
+                    int_pass(INT_EARLY + 5)
+                    flag2()
+
+                @pl.when(i == 1)
+                def _():
+                    int_take([(1, 3, 0), (2, 1, 0), (1, 3, 1), (2, 1, 1)], 1)
+
+                @pl.when(i == 2)
+                def _():
+                    int_take([(3, 2, 0), (3, 2, 1)], 1)
+
+    @pl.loop(EARLY // 2, CHUNKS // 2)
+    def _(i):
+        for odd, split, split_next in ((0, split_a, split_b), (1, split_b, split_a)):
+            c = 2 * i + odd
+
+            @pl.when(among(c, (6, 8, 9)))
+            def _():
+                tick(8 + after(c, (8, 9)))
+
+            @pl.when(among(c, (7, 8, 10, 11, 12, 14)))
+            def _():
+                arrive(7 + after(c, (8, 10, 11, 12, 14)))
+
+            later = jnp.minimum(c + 1, CHUNKS - 1)
+
+            @pl.loop(0, 2)
+            def _(n):
+                parts = [(n * 2 + k // 4, k % 4, n * 2048 + k * 256) for k in range(8)]
+                multiply(2 * c + n, c, n, split, split_next, later, parts)
 
     flag3()
     for slot in range(SLOTS):
@@ -806,7 +872,7 @@
             pltpu.VMEM((DEPTH, COLS), BF16),
             pltpu.VMEM((2 * CHUNK, DEPTH), BF16),
             pltpu.VMEM((2 * CHUNK, DEPTH), BF16),
-            pltpu.VMEM((SLOTS, 8, CHUNK // TILE, TILE, 128), F32),
+            pltpu.VMEM((SLOTS, 4, CHUNK // TILE, TILE, 128), F32),
             pltpu.VMEM((4, 4, 8, 128), jnp.int32),
             pltpu.VMEM((4, 2, 8, 128), jnp.int32),
             pltpu.VMEM((4, 2, 8, 128), jnp.int32),
@@ -838,12 +904,13 @@
 
 
 def shards(amplitudes, integrals, amp_mask, int_mask, occ_shift, virt_shift):
-    masks = jnp.stack([amp_mask.reshape(128), int_mask.reshape(128)])
+    halves = int_mask.reshape(8, 4, 2, 2).transpose(2, 0, 1, 3)
+    masks = jnp.stack([amp_mask.reshape(128), halves.reshape(128)])
     count = jnp.arange(128, dtype=jnp.int32)
     slots = jnp.sum(jnp.where(count[:, None] < count[None, :], masks[:, :, None], 0), axis=1)
     used = slots + masks
     room = jnp.array([STEP_TILES * n for n in NEED], jnp.int32)
-    over = jnp.any(used[0].reshape(CHUNKS, 8)[:, 7] > room) | (used[1, 127] > INT_MOST)
+    over = jnp.any(used[0].reshape(CHUNKS, 8)[:, 7] > room) | (used[1, 63] > 2 * INT_EARLY * INT_PIECE) | (used[1, 127] > INT_MOST)
     limit = jnp.array([[MOST - 1], [INT_MOST - 1]], jnp.int32)
     at = jnp.where(masks != 0, jnp.minimum(slots, limit), 0)
     kind = jnp.where(masks != 0, 1 + ((at ^ count[None, :]) & 1), 0)
@@ -854,7 +921,7 @@
     tables = jnp.stack([(at[0] >> 1) & 1, at[0] >> 2, kind[0], at[1] >> 1, kind[1], flags, flags, flags])
     a, b = place
     listing = jnp.stack([
-        a >> 2, 1 - ((a >> 1) & 1), (a >> 1) & 1, turn[0], b >> 5, (b >> 1) & 7, (b >> 4) & 1, turn[1]
+        a >> 2, 1 - ((a >> 1) & 1), (a >> 1) & 1, turn[0], (b >> 3) & 7, (b >> 1) & 3, b >> 6, turn[1]
     ])
     update, over = packed_ladder(amplitudes, integrals, tables, listing, occ_shift, virt_shift)
     return lax.cond(

time: 219 us -> 213 us (0.973)
  Pallas kernels: 202 us -> 197 us
    pallas_call x1, Pallas kernels: 202 us -> 197 us  [packed_ladder(): pl.pallas_call(packed_kernel, name='packed_ladder', out_shape=(jax.ShapeD...]
    unnamed x12 -> x13, local copies, waits for them, and re-layouts: 6.64 us -> 7.4 us
where the time goes in v3:
time: 213 us; the launch traced here: 212 us
  Pallas kernels  197 us (92%)
  local copies, waits for them, and re-layouts  10.9 us (5%)
  between operations  2.71 us (1%)
    pallas_call x1, Pallas kernels, packed_ladder(): pl.pallas_call(packed_kernel, name='packed_ladder', out_shape=(jax.ShapeD...  197 us
    unnamed x13, local copies, waits for them, and re-layouts  7.4 us

profile of v3, /device:TPU:1, one launch (start us, length us, event | category | flops | bytes accessed | tf_op | source)
XLA Modules:
  0.0 212.2 jit_solution(11753358947888455839)
XLA Ops:
  0.0 0.8 copy.22
  0.8 0.8 copy.21
  1.5 0.1 stack_reshape.6
  1.6 0.1 copy.23
  1.8 0.1 stack_reshape.7
  1.9 0.1 select_reduce_fusion.1
  2.1 0.6 fusion.4
  4.0 0.1 select_reduce_fusion
  4.2 0.6 stack.8.listing
  4.8 0.1 reshape_squeeze.3
  4.9 1.4 fusion.1
  7.0 0.6 stack.7.tables
  7.6 0.0 copy-start
  7.6 0.0 copy-start.1
  7.6 0.0 copy-start.2
  7.6 0.0 copy-start.3
  7.6 0.0 copy-start.4
  7.6 196.9 %packed_ladder.1 = (f32[256,64,128]{2,1,0:T(8,128)}, s32[8,128]{1,0:T(8,128)}, f32[2,4,4,26,64,128]{5,4,3,2,1,0:T(8,128)}, f32[8,52,64,128]{3,2,1,0:T(8,128)}) custom-call(f32[32,64,256]{2,1,0:T(8,128)} %bitcast.16, f32[512,1024]{1,0:T(8,128)} %ints.1, s32[8,128]{1,0:T(8,128)} %stack.7.tables, s32[8,128]{1,0:T(8,128)} %stack.8.listing, f32[16,128]{1,0:T(8,128)} %bitcast.14, ...), custom_call_target="tpu_custom_call" | custom-call | flops 51539607552 | bytes 83886080 | tf_op jit(solution)/shard_map/packed_ladder/pallas_call | solution.py:854
  204.5 1.2 slice.44
  206.3 0.0 copy-done
  206.3 0.0 copy-done.1
  206.3 0.0 copy-done.2
  206.4 0.0 copy-done.3
  206.4 0.0 copy-done.4
  206.4 5.9 %copy.29 = f32[16384,128]{1,0:T(8,128)} copy(f32[16384,128]{1,0:T(8,128)} %get-tuple-element.34) | data formatting | bytes 16777216
  (10 shorter events, 0.1 us)
Async XLA Ops:
  7.6 198.7 %copy-start = (s32[8,16]{1,0:T(8,128)S(1)}, s32[8,16]{1,0:T(8,128)}, u32[]{:S(2)}) copy-start(s32[8,16]{1,0:T(8,128)} %param.13) | copy-start | bytes 1540
  7.6 198.7 %copy-start.1 = (f32[2048]{0:T(1024)S(1)}, f32[2048]{0:T(1024)}, u32[]{:S(2)}) copy-start(f32[2048]{0:T(1024)} %param.14) | copy-start | bytes 24580
  7.6 198.8 %copy-start.2 = (s32[32,4]{0,1:T(4,128)S(1)}, s32[32,4]{0,1:T(4,128)}, u32[]{:S(2)}) copy-start(s32[32,4]{0,1:T(4,128)} %param.12) | copy-start | bytes 1540
  7.6 198.8 %copy-start.3 = (f32[2048,256]{1,0:T(8,128)S(1)}, f32[2048,256]{1,0:T(8,128)}, u32[]{:S(2)}) copy-start(f32[2048,256]{1,0:T(8,128)} %param.10) | copy-start | bytes 6291460
  7.6 198.8 %copy-start.4 = (f32[1024]{0:T(1024)S(1)}, f32[1024]{0:T(1024)}, u32[]{:S(2)}) copy-start(f32[1024]{0:T(1024)} %param.15) | copy-start | bytes 12292

commit v4 on v3

--- a/solution.py
+++ b/solution.py
@@ -344,7 +344,7 @@
 INT_PIECE = INT_PAIRS // INT_PIECES
 INT_EARLY = 7
 SLOTS = 8
-EARLY = 6
+EARLY = 4
 
 
 def packed_kernel(
@@ -532,10 +532,13 @@
             for e in (0, 1):
                 wait_bytes(bundle(way, 2, rows_of(c, e)), amp_recv.at[way, 3, e, c])
 
-    def tick(t):
-        for lead, step in ((8, step1), (6, step2), (4, step3), (2, step4)):
+    def tick(t, leads=(2, 4, 6, 8)):
+        for lead, step in zip(leads, (step4, step3, step2, step1)):
             c = t + lead
-            pl.when((c >= (8 if lead == 8 else 0)) & (c < STEPS))(functools.partial(step, c))
+            pl.when((c >= 0) & (c < STEPS))(functools.partial(step, c))
+
+    def brisk(t):
+        tick(t, (1, 2, 3, 5 if t >= 0 else STEPS + 3))
 
     def fetch(s):
         rows = rows_of(s)
@@ -629,7 +632,7 @@
                 tiles.append(both[:, :128] * listing[1, place].astype(F32) + both[:, 128:] * listing[2, place].astype(F32))
             own[way, i] = beside(*tiles, listing[3, 2 * pair], listing[3, 2 * pair + 1])
 
-    for c in range(8):
+    for c in range(5):
         step1(c)
     ring1()
 
@@ -658,23 +661,18 @@
     for way in (0, 1):
         pltpu.make_async_copy(own.at[way], whole_amps.at[way, z, x], local.at[way]).wait()
 
-    tick(-6)
+    brisk(-3)
     plane1()
-    tick(-5)
-    tick(-4)
+    ring3()
+    unpack_ints(own_ints, 0, 0, 0)
+    brisk(-2)
     plane2()
-    tick(-3)
-    ring3()
-    tick(-2)
-    unpack_ints(own_ints, 0, 0, 0)
     unpack_ints(own_ints, 0, 0, 1)
+    int_pass(0)
+    int_pass(1)
+    int_take([(0, 0, 1)], 0)
+    brisk(-1)
     plane3()
-    for p in range(2):
-        int_pass(p)
-    tick(-1)
-    int_take([(0, 0, 1)], 0)
-    plane4()
-    flag0()
 
     @pl.loop(2, INT_EARLY)
     def _(p):
@@ -684,25 +682,28 @@
     def _(p):
         int_start(p)
 
-    tick(0)
-    flag1()
+    brisk(0)
+    plane4()
+    flag0()
     int_take([(1, 3, 0), (2, 1, 0), (1, 3, 1), (2, 1, 1)], 0)
-    tick(1)
 
     @pl.loop(0, INT_EARLY)
     def _(p):
         int_far(p)
 
+    brisk(1)
+    flag1()
     int_take([(3, 2, 0), (3, 2, 1)], 0)
-    tick(2)
     arrive(0)
     arrive(1)
 
-    @pl.loop(INT_EARLY, INT_EARLY + 3)
+    @pl.loop(INT_EARLY, INT_EARLY + 2)
     def _(p):
         int_pass(p)
 
-    tick(3)
+    step2(5)
+    step1(7)
+    step1(8)
 
     def stage_wait(slot):
         wait_bytes(stage.at[slot, pl.ds(0, 3)], out_send.at[slot])
@@ -774,39 +775,37 @@
             n = unit // EARLY
             c = unit - n * EARLY
 
-            @pl.when(among(unit, (3, 4, 7, 10)))
+            @pl.when(among(unit, (1, 2, 4, 6)))
             def _():
-                tick(4 + after(unit, (4, 7, 10)))
-
-            @pl.when(among(unit, (1, 2, 3, 4, 11)))
+                tick(1 + after(unit, (2, 4, 6)))
+
+            @pl.when(among(unit, (1, 2, 5, 7)))
             def _():
-                arrive(jnp.where(unit == 11, 6, unit + 1))
+                arrive(2 + after(unit, (2, 5, 7)))
 
             later = jnp.where((unit == EARLY - 1), 0, c + 1)
             multiply(unit, c, n, split, split_next, later, everything)
             if odd == 0:
                 @pl.when(i == 0)
                 def _():
+                    int_pass(INT_EARLY + 2)
                     int_pass(INT_EARLY + 3)
+                    step3(4)
+                    step2(6)
+            else:
+                @pl.when(i == 0)
+                def _():
                     int_pass(INT_EARLY + 4)
-
-                @pl.when(i == 2)
+                    int_pass(INT_EARLY + 5)
+                    flag2()
+                    int_take([(1, 3, 0), (2, 1, 0), (1, 3, 1), (2, 1, 1)], 1)
+
+                @pl.when(i == 1)
                 def _():
                     @pl.loop(INT_EARLY, INT_PIECES)
                     def _(p):
                         int_far(p)
-            else:
-                @pl.when(i == 0)
-                def _():
-                    int_pass(INT_EARLY + 5)
-                    flag2()
-
-                @pl.when(i == 1)
-                def _():
-                    int_take([(1, 3, 0), (2, 1, 0), (1, 3, 1), (2, 1, 1)], 1)
-
-                @pl.when(i == 2)
-                def _():
+
                     int_take([(3, 2, 0), (3, 2, 1)], 1)
 
     @pl.loop(EARLY // 2, CHUNKS // 2)
@@ -814,13 +813,13 @@
         for odd, split, split_next in ((0, split_a, split_b), (1, split_b, split_a)):
             c = 2 * i + odd
 
-            @pl.when(among(c, (6, 8, 9)))
+            @pl.when(among(c, (5, 6, 8, 10, 11, 13)))
             def _():
-                tick(8 + after(c, (8, 9)))
-
-            @pl.when(among(c, (7, 8, 10, 11, 12, 14)))
+                tick(5 + after(c, (6, 8, 10, 11, 13)))
+
+            @pl.when(among(c, (5, 7, 8, 10, 11, 12, 14)))
             def _():
-                arrive(7 + after(c, (8, 10, 11, 12, 14)))
+                arrive(6 + after(c, (7, 8, 10, 11, 12, 14)))
 
             later = jnp.minimum(c + 1, CHUNKS - 1)
 

time: 213 us -> 202 us (0.948)
  Pallas kernels: 197 us -> 185 us
    pallas_call x1, Pallas kernels: 197 us -> 185 us  [packed_ladder(): pl.pallas_call(packed_kernel, name='packed_ladder', out_shape=(jax.ShapeD...]
where the time goes in v4:
time: 202 us; the launch traced here: 201 us
  Pallas kernels  185 us (92%)
  local copies, waits for them, and re-layouts  10.9 us (5%)
  between operations  2.71 us (1%)
    pallas_call x1, Pallas kernels, packed_ladder(): pl.pallas_call(packed_kernel, name='packed_ladder', out_shape=(jax.ShapeD...  185 us
    unnamed x13, local copies, waits for them, and re-layouts  7.4 us

profile of v4, /device:TPU:1, one launch (start us, length us, event | category | flops | bytes accessed | tf_op | source)
XLA Modules:
  0.0 200.6 jit_solution(11278788961988781855)
XLA Ops:
  0.0 0.8 copy.22
  0.8 0.8 copy.21
  1.5 0.1 stack_reshape.6
  1.6 0.1 copy.23
  1.8 0.1 stack_reshape.7
  1.9 0.1 select_reduce_fusion.1
  2.1 0.6 fusion.4
  4.0 0.1 select_reduce_fusion
  4.2 0.6 stack.8.listing
  4.8 0.1 reshape_squeeze.3
  4.9 1.4 fusion.1
  7.0 0.6 stack.7.tables
  7.6 0.0 copy-start
  7.6 0.0 copy-start.1
  7.6 0.0 copy-start.2
  7.6 0.0 copy-start.3
  7.6 0.0 copy-start.4
  7.6 185.2 %packed_ladder.1 = (f32[256,64,128]{2,1,0:T(8,128)}, s32[8,128]{1,0:T(8,128)}, f32[2,4,4,26,64,128]{5,4,3,2,1,0:T(8,128)}, f32[8,52,64,128]{3,2,1,0:T(8,128)}) custom-call(f32[32,64,256]{2,1,0:T(8,128)} %bitcast.16, f32[512,1024]{1,0:T(8,128)} %ints.1, s32[8,128]{1,0:T(8,128)} %stack.7.tables, s32[8,128]{1,0:T(8,128)} %stack.8.listing, f32[16,128]{1,0:T(8,128)} %bitcast.14, ...), custom_call_target="tpu_custom_call" | custom-call | flops 51539607552 | bytes 83886080 | tf_op jit(solution)/shard_map/packed_ladder/pallas_call | solution.py:853
  192.8 1.2 slice.44
  194.6 0.0 copy-done
  194.6 0.0 copy-done.1
  194.7 0.0 copy-done.2
  194.7 0.0 copy-done.3
  194.7 0.0 copy-done.4
  194.7 5.9 %copy.29 = f32[16384,128]{1,0:T(8,128)} copy(f32[16384,128]{1,0:T(8,128)} %get-tuple-element.34) | data formatting | bytes 16777216
  (10 shorter events, 0.1 us)
Async XLA Ops:
  7.6 187.1 %copy-start = (s32[8,16]{1,0:T(8,128)S(1)}, s32[8,16]{1,0:T(8,128)}, u32[]{:S(2)}) copy-start(s32[8,16]{1,0:T(8,128)} %param.13) | copy-start | bytes 1540
  7.6 187.1 %copy-start.1 = (f32[2048]{0:T(1024)S(1)}, f32[2048]{0:T(1024)}, u32[]{:S(2)}) copy-start(f32[2048]{0:T(1024)} %param.14) | copy-start | bytes 24580
  7.6 187.1 %copy-start.2 = (s32[32,4]{0,1:T(4,128)S(1)}, s32[32,4]{0,1:T(4,128)}, u32[]{:S(2)}) copy-start(s32[32,4]{0,1:T(4,128)} %param.12) | copy-start | bytes 1540
  7.6 187.1 %copy-start.3 = (f32[2048,256]{1,0:T(8,128)S(1)}, f32[2048,256]{1,0:T(8,128)}, u32[]{:S(2)}) copy-start(f32[2048,256]{1,0:T(8,128)} %param.10) | copy-start | bytes 6291460
  7.6 187.1 %copy-start.4 = (f32[1024]{0:T(1024)S(1)}, f32[1024]{0:T(1024)}, u32[]{:S(2)}) copy-start(f32[1024]{0:T(1024)} %param.15) | copy-start | bytes 12292

commit v5 on v4

--- a/solution.py
+++ b/solution.py
@@ -817,16 +817,14 @@
             def _():
                 tick(5 + after(c, (6, 8, 10, 11, 13)))
 
+            later = jnp.minimum(c + 1, CHUNKS - 1)
+            multiply(2 * c, c, 0, split, split_next, later, [])
+
             @pl.when(among(c, (5, 7, 8, 10, 11, 12, 14)))
             def _():
                 arrive(6 + after(c, (7, 8, 10, 11, 12, 14)))
 
-            later = jnp.minimum(c + 1, CHUNKS - 1)
-
-            @pl.loop(0, 2)
-            def _(n):
-                parts = [(n * 2 + k // 4, k % 4, n * 2048 + k * 256) for k in range(8)]
-                multiply(2 * c + n, c, n, split, split_next, later, parts)
+            multiply(2 * c + 1, c, 1, split, split_next, later, everything)
 
     flag3()
     for slot in range(SLOTS):

time: 202 us -> 199 us (0.985)
  Pallas kernels: 185 us -> 182 us
    pallas_call x1, Pallas kernels: 185 us -> 182 us  [packed_ladder(): pl.pallas_call(packed_kernel, name='packed_ladder', out_shape=(jax.ShapeD...]
where the time goes in v5:
time: 199 us; the launch traced here: 198 us
  Pallas kernels  182 us (91%)
  local copies, waits for them, and re-layouts  10.9 us (5%)
  between operations  2.71 us (1%)
    pallas_call x1, Pallas kernels, packed_ladder(): pl.pallas_call(packed_kernel, name='packed_ladder', out_shape=(jax.ShapeD...  182 us
    unnamed x13, local copies, waits for them, and re-layouts  7.4 us

profile of v5, /device:TPU:1, one launch (start us, length us, event | category | flops | bytes accessed | tf_op | source)
XLA Modules:
  0.0 197.7 jit_solution(6379986369097847676)
XLA Ops:
  0.0 0.8 copy.22
  0.8 0.8 copy.21
  1.5 0.1 stack_reshape.6
  1.6 0.1 copy.23
  1.8 0.1 stack_reshape.7
  1.9 0.1 select_reduce_fusion.1
  2.1 0.6 fusion.4
  4.0 0.1 select_reduce_fusion
  4.2 0.6 stack.8.listing
  4.8 0.1 reshape_squeeze.3
  4.9 1.4 fusion.1
  7.0 0.6 stack.7.tables
  7.6 0.0 copy-start
  7.6 0.0 copy-start.1
  7.6 0.0 copy-start.2
  7.6 0.0 copy-start.3
  7.6 0.0 copy-start.4
  7.6 182.3 %packed_ladder.1 = (f32[256,64,128]{2,1,0:T(8,128)}, s32[8,128]{1,0:T(8,128)}, f32[2,4,4,26,64,128]{5,4,3,2,1,0:T(8,128)}, f32[8,52,64,128]{3,2,1,0:T(8,128)}) custom-call(f32[32,64,256]{2,1,0:T(8,128)} %bitcast.16, f32[512,1024]{1,0:T(8,128)} %ints.1, s32[8,128]{1,0:T(8,128)} %stack.7.tables, s32[8,128]{1,0:T(8,128)} %stack.8.listing, f32[16,128]{1,0:T(8,128)} %bitcast.14, ...), custom_call_target="tpu_custom_call" | custom-call | flops 51539607552 | bytes 83886080 | tf_op jit(solution)/shard_map/packed_ladder/pallas_call | solution.py:851
  189.9 1.2 slice.44
  191.7 0.0 copy-done
  191.8 0.0 copy-done.1
  191.8 0.0 copy-done.2
  191.8 0.0 copy-done.3
  191.8 0.0 copy-done.4
  191.8 5.9 %copy.29 = f32[16384,128]{1,0:T(8,128)} copy(f32[16384,128]{1,0:T(8,128)} %get-tuple-element.34) | data formatting | bytes 16777216
  (10 shorter events, 0.1 us)
Async XLA Ops:
  7.6 184.2 %copy-start = (s32[8,16]{1,0:T(8,128)S(1)}, s32[8,16]{1,0:T(8,128)}, u32[]{:S(2)}) copy-start(s32[8,16]{1,0:T(8,128)} %param.13) | copy-start | bytes 1540
  7.6 184.2 %copy-start.1 = (f32[2048]{0:T(1024)S(1)}, f32[2048]{0:T(1024)}, u32[]{:S(2)}) copy-start(f32[2048]{0:T(1024)} %param.14) | copy-start | bytes 24580
  7.6 184.2 %copy-start.2 = (s32[32,4]{0,1:T(4,128)S(1)}, s32[32,4]{0,1:T(4,128)}, u32[]{:S(2)}) copy-start(s32[32,4]{0,1:T(4,128)} %param.12) | copy-start | bytes 1540
  7.6 184.2 %copy-start.3 = (f32[2048,256]{1,0:T(8,128)S(1)}, f32[2048,256]{1,0:T(8,128)}, u32[]{:S(2)}) copy-start(f32[2048,256]{1,0:T(8,128)} %param.10) | copy-start | bytes 6291460
  7.6 184.2 %copy-start.4 = (f32[1024]{0:T(1024)S(1)}, f32[1024]{0:T(1024)}, u32[]{:S(2)}) copy-start(f32[1024]{0:T(1024)} %param.15) | copy-start | bytes 12292
